TPU v7x, 32 devices: a whole 2x2x4 slice. The times are simulated.
32 devices in a mesh: resp: 8 (over z, core), head: 4 (over y, x).
Axes of the slice: x: 2, y: 2, z: 4, core: 2. Of those that a mesh axis runs over, the one named last changes fastest.
Arguments:
- q_nope: bfloat16 [2048, 8192], P('resp', 'head'), may hold values from -6 to 6
- q_rope: bfloat16 [2048, 4096], P('resp', 'head'), may hold values from -160 to 160
- latents: bfloat16 [256, 576], P('resp'), may hold values from -4.1 to 4.1
- w_uk: bfloat16 [64, 128, 512], P('head'), may hold values from -0.25 to 0.25
- w_uv: bfloat16 [64, 512, 128], P('head'), may hold values from -0.25 to 0.25
- grad_out: bfloat16 [2048, 8192], P('resp', 'head'), may hold values from -6 to 6
- prompt_of: int32 [8, 4], P('resp'), may hold values from 0 to 7
- live_rows: int32 [8, 4], P('resp'), may hold values from 1 to 64, 172 in all within a row
- prompt_block: int32 [8], replicated, may hold values from 0 to 7, each once
Outputs:
- d_q_nope: bfloat16 [2048, 8192], P('resp', 'head')
- d_q_rope: bfloat16 [2048, 4096], P('resp', 'head')
- d_latents: float32 [256, 576], P('resp')
- d_w_uk: bfloat16 [64, 128, 512], P('head')
- d_w_uv: bfloat16 [64, 512, 128], P('head')
Inputs may be any that keep to these rules, and one draw needn't show every extreme that they name: `live_rows`: live rows of a stretch come first; the stretches of one index of resp hold 172 live rows together, one stretch of them full. `prompt_block`: each block is named once.
All inputs are finite; a program needn't handle non-finite values.
Results may differ from a plain program's by a relative error of at most 0.0068.
Values may be sent and summed in bfloat16 or wider, within the bound.
A program may use at most 64 MiB of HBM per device.

v0:
```python
import jax
import jax.numpy as jnp
from jax import lax
from jax.sharding import PartitionSpec as P

LAT = 512
ROPE = 64
HD = 128
ROWS = 64
P_SIZE = 32


def per_device(q_nope, q_rope, latents, w_uk, w_uv, grad_out, prompt_of, live_rows, prompt_block):
    heads = w_uk.shape[0]
    stretches = prompt_of.shape[1]
    scale = (HD + ROPE) ** (-0.5)
    gathered = lax.all_gather(latents, "resp", axis=0, tiled=True)
    num_blocks = gathered.shape[0] // P_SIZE
    table = gathered.reshape(num_blocks, P_SIZE, LAT + ROPE)
    blocks = prompt_block[prompt_of[0]]
    keys = jnp.take(table, blocks, axis=0)
    latent_part = keys[..., :LAT]
    query_nope = q_nope.reshape(stretches, ROWS, heads, HD)
    query_rope = q_rope.reshape(stretches, ROWS, heads, ROPE)
    live = lax.broadcasted_iota(jnp.int32, (stretches, ROWS), 1) < live_rows[0][:, None]
    grad_rows = jnp.where(
        live[:, :, None, None],
        grad_out.reshape(stretches, ROWS, heads, HD),
        jnp.zeros((), jnp.bfloat16),
    )
    q_abs = jnp.einsum(
        "crhd,hdl->crhl", query_nope, w_uk, preferred_element_type=jnp.float32
    ).astype(jnp.bfloat16)
    q_cat = jnp.concatenate([q_abs, query_rope], axis=-1)
    scores = jnp.einsum("crhk,cpk->chrp", q_cat, keys, preferred_element_type=jnp.float32) * scale
    probs = jax.nn.softmax(scores, axis=-1)
    probs_low = probs.astype(jnp.bfloat16)
    out_lat = jnp.einsum(
        "chrp,cpl->crhl", probs_low, latent_part, preferred_element_type=jnp.float32
    ).astype(jnp.bfloat16)
    d_out = jnp.einsum(
        "crhd,hld->crhl", grad_rows, w_uv, preferred_element_type=jnp.float32
    ).astype(jnp.bfloat16)
    grad_uv = jnp.einsum("crhl,crhd->hld", out_lat, grad_rows, preferred_element_type=jnp.float32)
    d_probs = jnp.einsum("crhl,cpl->chrp", d_out, latent_part, preferred_element_type=jnp.float32)
    delta = jnp.sum(probs * d_probs, axis=-1, keepdims=True)
    d_scores = (probs * (d_probs - delta)).astype(jnp.bfloat16)
    d_full = (
        jnp.einsum("chrp,cpk->crhk", d_scores, keys, preferred_element_type=jnp.float32) * scale
    )
    d_abs = d_full[..., :LAT].astype(jnp.bfloat16)
    d_rope = d_full[..., LAT:].astype(jnp.bfloat16)
    d_keys = (
        jnp.einsum("chrp,crhk->cpk", d_scores, q_cat, preferred_element_type=jnp.float32) * scale
    )
    d_vals = jnp.einsum("chrp,crhl->cpl", probs_low, d_out, preferred_element_type=jnp.float32)
    d_keys = d_keys + jnp.pad(d_vals, ((0, 0), (0, 0), (0, ROPE)))
    selector = (blocks[:, None] == jnp.arange(num_blocks, dtype=jnp.int32)[None, :]).astype(
        jnp.float32
    )
    partial_rows = jnp.einsum(
        "cn,cpk->npk", selector, d_keys, precision=lax.Precision.HIGHEST
    ).reshape(num_blocks * P_SIZE, LAT + ROPE)
    d_nope = jnp.einsum("crhl,hdl->crhd", d_abs, w_uk, preferred_element_type=jnp.float32).astype(
        jnp.bfloat16
    )
    grad_uk = jnp.einsum("crhd,crhl->hdl", query_nope, d_abs, preferred_element_type=jnp.float32)
    holder_rows = lax.psum_scatter(partial_rows, "resp", scatter_dimension=0, tiled=True)
    grad_lat = lax.psum(holder_rows, "head")
    summed = lax.psum((grad_uk, grad_uv), "resp")
    final_uk = summed[0].astype(jnp.bfloat16)
    final_uv = summed[1].astype(jnp.bfloat16)
    return (
        d_nope.reshape(stretches * ROWS, heads * HD),
        d_rope.reshape(stretches * ROWS, heads * ROPE),
        grad_lat,
        final_uk,
        final_uv,
    )


def solution(mesh):
    in_specs = (
        P("resp", "head"),
        P("resp", "head"),
        P("resp", None),
        P("head", None, None),
        P("head", None, None),
        P("resp", "head"),
        P("resp", None),
        P("resp", None),
        P(),
    )
    out_specs = (
        P("resp", "head"),
        P("resp", "head"),
        P("resp", None),
        P("head", None, None),
        P("head", None, None),
    )
    return jax.shard_map(
        per_device, mesh=mesh, in_specs=in_specs, out_specs=out_specs, check_vma=False
    )
```

profile of v0, /device:TPU:0, one launch (start us, length us, event | category | flops | bytes accessed | tf_op | source)
XLA Modules:
  0.0 299.0 jit_solution(14005498751307574652)
XLA Ops:
  7.2 0.0 copy-start
  7.2 0.0 reduce-scatter.2.cloned.1.call-start
  7.2 0.8 fusion.65
  8.0 1.3 gather_fusion
  9.3 0.7 iota_compare_fusion.1
  10.1 16.2 %all_gather.3 = bf16[256,576]{1,0:T(8,128)(2,1)S(1)} all-gather(bf16[32,576]{1,0:T(8,128)(2,1)} %param.11), channel_id=1, replica_groups=mesh['resp'=8,'head'=4] {'resp'}, dimensions={0}, use_global_device_ids=true | all-gather | bytes 331776 | tf_op jit(solution)/shard_map/all_gather | solution.py:17
  26.3 1.4 copy.45
  27.8 1.2 copy.22
  29.0 2.5 reshape.105
  31.5 2.6 copy.23
  34.0 2.4 copy.46
  36.4 0.0 copy-done
  36.4 0.0 copy-done.4
  36.4 1.2 fusion.78
  37.7 2.6 convert_bitcast_fusion.1
  40.3 1.2 gather_fusion.1
  41.5 1.0 broadcast_select_fusion
  42.5 5.2 %convert_bitcast_fusion = bf16[4,64,16,512]{3,1,0,2:T(8,128)(2,1)} fusion(bf16[16,512,128]{2,1,0:T(8,128)(2,1)} %param.13, bf16[4,64,16,128]{3,2,1,0:T(8,128)(2,1)} %bitcast.107, pred[4,64]{1,0:T(4,128)(4,1)S(1)} %iota_compare_fusion.1), kind=kOutput, calls=%fused_computation.15 | convolution fusion | flops 539492352 | bytes 7340288 | tf_op jit(solution)/shard_map/crhd,hld->crhl/dot_general | solution.py:41
  47.7 6.4 %fusion.73 = (f32[4,16,64]{2,1,0:T(8,128)S(1)}, f32[4,16,64,32]{2,3,1,0:T(8,128)}) fusion(bf16[4,32,576]{2,1,0:T(8,128)(2,1)S(1)} %broadcast_select_fusion, bf16[4,64,16,64]{3,1,0,2:T(8,128)(2,1)} %copy.23, bf16[4,64,16,512]{3,1,0,2:T(8,128)(2,1)} %convert_bitcast_fusion.1), kind=kOutput, calls=%fused_computation.74 | convolution fusion | flops 160825376 | bytes 5406720 | tf_op jit(solution)/shard_map/sub | solution.py:36
  54.1 4.7 %multiply_reduce_fusion = (f32[4,16,64]{2,1,0:T(8,128)S(1)}, f32[4,16,64,32]{2,3,1,0:T(8,128)S(1)}) fusion(f32[4,16,64,32]{2,3,1,0:T(8,128)} %get-tuple-element.20, f32[4,16,64]{2,1,0:T(8,128)S(1)} %get-tuple-element.19, bf16[4,64,16,512]{3,1,0,2:T(8,128)(2,1)} %convert_bitcast_fusion, bf16[4,32,576]{2,1,0:T(8,128)(2,1)S(1)} %broadcast_select_fusion), kind=kOutput, calls=%fused_computation.37 | convolution fusion | flops 134606848 | bytes 5423104 | tf_op jit(solution)/shard_map/crhl,cpl->chrp/dot_general | solution.py:45
  58.8 0.3 fusion.71
  59.2 0.0 copy-start.5
  59.2 0.0 copy-start.9
  59.2 1.2 fusion.2
  60.5 0.0 copy-done.5
  60.5 0.0 copy-done.9
  60.5 1.3 copy-done.3
  61.7 0.8 fusion.11
  62.6 0.2 copy.87
  62.8 0.7 fusion.49
  63.5 1.0 copy.30
  64.5 0.0 reduce-scatter.2.cloned.1.call-update
  64.5 0.2 all-reduce.5.cloned.1.call-start
  64.7 5.9 %fusion.17 = f32[16,512,128]{2,1,0:T(8,128)} fusion(bf16[4,64,16,128]{3,2,1,0:T(8,128)(2,1)} %bitcast.108, pred[4,64]{1,0:T(4,128)(4,1)S(1)} %iota_compare_fusion.1, bf16[4,16,64,32]{2,3,1,0:T(8,128)(2,1)} %copy-done.9, bf16[4,32,576]{2,1,0:T(8,128)(2,1)S(1)} %broadcast_select_fusion), kind=kOutput, calls=%fused_computation.22 | convolution fusion | flops 673710080 | bytes 5636608 | tf_op jit(solution)/shard_map/crhl,crhd->hld/dot_general | solution.py:44
  70.6 2.6 fusion.1
  73.3 2.3 copy-done.1
  75.5 3.5 %convolution_bitcast_fusion = f32[16,128,512]{1,2,0:T(8,128)} fusion(bf16[4,64,16,128]{3,2,1,0:T(8,128)(2,1)S(1)} %bitcast.105, bf16[4,64,16,576]{3,1,2,0:T(8,128)(2,1)S(1)} %fusion.1), kind=kOutput, calls=%fused_computation.23 | convolution fusion | flops 536870912 | bytes 9437184 | tf_op jit(solution)/shard_map/crhd,crhl->hdl/dot_general | solution.py:67
  79.1 171.4 %all-reduce.6 = (bf16[16,128,512]{1,2,0:T(8,128)(2,1)}, bf16[16,512,128]{2,1,0:T(8,128)(2,1)}) all-reduce(f32[16,128,512]{1,2,0:T(8,128)} %convolution_bitcast_fusion, f32[16,512,128]{2,1,0:T(8,128)} %fusion.17), channel_id=1, replica_groups=mesh['resp'=8,'head'=4] {'resp'}, use_global_device_ids=true, to_apply=%region_5.6 | all-reduce | flops 2097152 | bytes 12582912 | tf_op jit(solution)/shard_map/psum | solution.py:70
  250.5 0.0 all-reduce.5.cloned.1.call-update
  250.6 0.0 slice-start
  250.6 4.5 %fusion.31 = bf16[4,64,16,128]{3,1,0,2:T(8,128)(2,1)} fusion(bf16[16,128,512]{2,1,0:T(8,128)(2,1)S(1)} %copy-done, bf16[4,64,16,576]{3,1,2,0:T(8,128)(2,1)} %copy-done.1), kind=kOutput, calls=%fused_computation.29 | convolution fusion | flops 537395200 | bytes 7340032 | tf_op jit(solution)/shard_map/crhl,hdl->crhd/dot_general | solution.py:64
  255.1 0.7 copy.29
  255.7 1.5 reshape.108
  257.3 4.0 %copy.33 = bf16[16,128,512]{2,1,0:T(8,128)(2,1)} copy(bf16[16,128,512]{1,2,0:T(8,128)(2,1)} %get-tuple-element.15) | data formatting | bytes 4194304
  261.3 0.7 copy.28
  261.9 1.2 copy.86
  263.2 27.4 %all-reduce.5.cloned.1.call-done = f32[32,576]{1,0:T(8,128)} async-done(((f32[32,576]{1,0:T(8,128)}), f32[32,576]{1,0:T(8,128)}) %all-reduce.5.cloned.1.call-update) | async-done | bytes 73744 | tf_op jit(solution)/shard_map/psum | solution.py:69
  290.6 1.5 copy.93
  (17 shorter events, 0.1 us)
Async XLA Ops:
  7.2 29.3 %copy-start = (bf16[16,128,512]{2,1,0:T(8,128)(2,1)S(1)}, bf16[16,128,512]{2,1,0:T(8,128)(2,1)}, u32[]{:S(2)}) copy-start(bf16[16,128,512]{2,1,0:T(8,128)(2,1)} %param.12) | copy-start | bytes 6291460
  7.2 243.3 %reduce-scatter.2.cloned.1.call-start = ((), (), s32[]{:S(2)}) async-start(), calls=%async_computation.1 | async-start | bytes 737280 | tf_op jit(solution)/shard_map/reduce_scatter | solution.py:68
  31.5 5.0 %copy-start.4 = (bf16[4,64,16,128]{3,1,0,2:T(8,128)(2,1)S(1)}, bf16[4,64,16,128]{3,1,0,2:T(8,128)(2,1)}, u32[]{:S(2)}) copy-start(bf16[4,64,16,128]{3,1,0,2:T(8,128)(2,1)} %copy.22) | copy-start | bytes 3145732
  54.1 4.7 %copy-start.6 = (f32[4,16,64,32]{2,3,1,0:T(8,128)S(1)}, f32[4,16,64,32]{2,3,1,0:T(8,128)}, u32[]{:S(2)}) copy-start(f32[4,16,64,32]{2,3,1,0:T(8,128)} %get-tuple-element.20) | copy-start | bytes 1572868
  54.1 5.0 %copy-start.2 = (bf16[4,64,16,512]{3,1,0,2:T(8,128)(2,1)S(1)}, bf16[4,64,16,512]{3,1,0,2:T(8,128)(2,1)}, u32[]{:S(2)}) copy-start(bf16[4,64,16,512]{3,1,0,2:T(8,128)(2,1)} %convert_bitcast_fusion.1) | copy-start | bytes 12582916
  54.1 5.1 %copy-start.7 = (bf16[4,64,16,64]{3,1,0,2:T(8,128)(2,1)S(1)}, bf16[4,64,16,64]{3,1,0,2:T(8,128)(2,1)}, u32[]{:S(2)}) copy-start(bf16[4,64,16,64]{3,1,0,2:T(8,128)(2,1)} %copy.23) | copy-start | bytes 1572868
  59.2 1.3 copy-start.5
  59.2 1.3 copy-start.9
  59.2 2.5 copy-start.3
  64.5 226.1 %all-reduce.5.cloned.1.call-start = ((), (), s32[]{:S(2)}) async-start(), calls=%async_computation.2 | async-start | bytes 163840 | tf_op jit(solution)/shard_map/psum | solution.py:69
  73.2 2.3 copy-start.1
  250.6 4.5 %slice-start = ((bf16[4,64,16,576]{3,1,2,0:T(8,128)(2,1)}), bf16[4,64,16,64]{3,1,2,0:T(8,128)(2,1)S(1)}, s32[]{:S(2)}) async-start(bf16[4,64,16,576]{3,1,2,0:T(8,128)(2,1)} %copy-done.1), calls=%async_computation.3 | async-start | bytes 2097152 | tf_op jit(solution)/shard_map/slice | solution.py:52
  257.3 4.0 %copy-start.8 = (bf16[4,64,16,128]{3,1,0,2:T(8,128)(2,1)S(1)}, bf16[4,64,16,128]{3,1,0,2:T(8,128)(2,1)}, u32[]{:S(2)}) copy-start(bf16[4,64,16,128]{3,1,0,2:T(8,128)(2,1)} %fusion.31) | copy-start | bytes 3145732
Sparse Core Ops, SparseCore 0:
  64.6 33.5 reduce-scatter.1
  250.7 39.8 all-reduce.4
where the time goes:
time: 300 us; the launch traced here: 299 us
  blocking collectives  188 us (63%)
  matrix products  36.9 us (12%)
  waiting for transfers between devices  27.5 us (9%)
  local copies, waits for them, and re-layouts  27 us (9%)
  between operations  14.2 us (5%)
  other arithmetic  5.47 us (2%)
    psum x1, blocking collectives, per_device(): summed = lax.psum((grad_uk, grad_uv), 'resp')  171 us
    psum x1, waiting for transfers between devices, per_device(): grad_lat = lax.psum(holder_rows, 'head')  27.4 us
    all_gather x1, blocking collectives, per_device(): gathered = lax.all_gather(latents, 'resp', axis=0, tiled=True)  16.2 us
    unnamed x25, local copies, waits for them, and re-layouts  14.2 us
    sub x1, matrix products, per_device(): probs = jax.nn.softmax(scores, axis=-1)  6.41 us
  transfers between devices with their start and end apart: 2, of which 1 were waited for; matrix products, arithmetic and copies ran while one was open for 8% of the time, Pallas kernels for 0%

commit v1 on v0

v1 whole, which is shorter than its diff:
```python
import functools

import jax
import jax.numpy as jnp
from jax import lax
from jax.experimental import pallas as pl
from jax.experimental.pallas import tpu as pltpu
from jax.sharding import PartitionSpec as P

LAT = 512
ROPE = 64
HD = 128
ROWS = 64
P_SIZE = 32
SCALE = (HD + ROPE) ** (-0.5)
BF = jnp.bfloat16
F32 = jnp.float32


def dot_nn(a, b):
    return lax.dot_general(a, b, (((1,), (0,)), ((), ())), preferred_element_type=F32)


def dot_nt(a, b):
    return lax.dot_general(a, b, (((1,), (1,)), ((), ())), preferred_element_type=F32)


def dot_tn(a, b):
    return lax.dot_general(a, b, (((0,), (0,)), ((), ())), preferred_element_type=F32)


def local_kernel(
    live_ref, qn_ref, qr_ref, go_ref, wk_ref, wv_ref, lat_ref, rope_ref,
    dqn_ref, dqr_ref, dkv_ref, dc_ref, dr_ref,
):
    tokens = qn_ref.shape[0]
    keys = lat_ref.shape[0]
    stretches = keys // P_SIZE
    row = lax.broadcasted_iota(jnp.int32, (tokens, keys), 0)
    lane = lax.broadcasted_iota(jnp.int32, (tokens, keys), 1)
    own = (row // ROWS) == (lane // P_SIZE)
    row_h = lax.broadcasted_iota(jnp.int32, (tokens, HD), 0)
    limit = jnp.zeros((tokens, HD), jnp.int32)
    for c in range(stretches):
        limit = jnp.where(row_h // ROWS == c, live_ref[c], limit)
    live = (row_h % ROWS) < limit
    lat = lat_ref[...]
    qr = qr_ref[...]
    dqr = jnp.zeros((tokens, 2 * ROPE), F32)
    dc = jnp.zeros((keys, LAT), F32)

    @pl.when(pl.program_id(0) == 0)
    def _():
        dc_ref[...] = jnp.zeros_like(dc_ref)
        dr_ref[...] = jnp.zeros_like(dr_ref)

    for i in range(2):
        cols = slice(i * HD, (i + 1) * HD)
        qn = qn_ref[:, cols]
        g = jnp.where(live, go_ref[:, cols], jnp.zeros((), BF))
        kn = dot_nt(lat, wk_ref[i]).astype(BF)
        vn = dot_nn(lat, wv_ref[i]).astype(BF)
        rope = rope_ref[i]
        s = dot_nt(
            jnp.concatenate([qn, qr], axis=1), jnp.concatenate([kn, rope], axis=1)
        ) * SCALE
        s = jnp.where(own, s, -jnp.inf)
        e = jnp.exp(s - jnp.max(s, axis=1, keepdims=True))
        p = e / jnp.sum(e, axis=1, keepdims=True)
        pb = p.astype(BF)
        dp = dot_nt(g, vn)
        delta = jnp.sum(p * dp, axis=1, keepdims=True)
        ds = (p * (dp - delta)).astype(BF)
        dqn_ref[:, cols] = (dot_nn(ds, kn) * SCALE).astype(BF)
        dqr = dqr + dot_nn(ds, rope)
        dk = (dot_tn(ds, qn) * SCALE).astype(BF)
        dv = dot_tn(pb, g).astype(BF)
        dkv_ref[2 * i] = dk
        dkv_ref[2 * i + 1] = dv
        dc = dc + dot_nn(dk, wk_ref[i]) + dot_nt(dv, wv_ref[i])
        dr_ref[i] += dot_tn(ds, qr) * SCALE
    dqr_ref[...] = (dqr * SCALE).astype(BF)
    dc_ref[...] += dc


def local_part(live, qn, qr, go, wk, wv, lat, rope2):
    heads = wk.shape[0]
    tokens = qn.shape[0]
    keys = lat.shape[0]
    full = lambda *shape: pl.BlockSpec(shape, lambda i: (0,) * len(shape))
    return pl.pallas_call(
        local_kernel,
        grid=(heads // 2,),
        in_specs=[
            pl.BlockSpec(memory_space=pltpu.SMEM),
            pl.BlockSpec((tokens, 2 * HD), lambda i: (0, i)),
            pl.BlockSpec((tokens, 2 * ROPE), lambda i: (0, i)),
            pl.BlockSpec((tokens, 2 * HD), lambda i: (0, i)),
            pl.BlockSpec((2, HD, LAT), lambda i: (i, 0, 0)),
            pl.BlockSpec((2, LAT, HD), lambda i: (i, 0, 0)),
            full(keys, LAT),
            full(2, keys, 2 * ROPE),
        ],
        out_specs=[
            pl.BlockSpec((tokens, 2 * HD), lambda i: (0, i)),
            pl.BlockSpec((tokens, 2 * ROPE), lambda i: (0, i)),
            pl.BlockSpec((4, keys, HD), lambda i: (i, 0, 0)),
            full(keys, LAT),
            full(2, keys, 2 * ROPE),
        ],
        out_shape=[
            jax.ShapeDtypeStruct((tokens, heads * HD), BF),
            jax.ShapeDtypeStruct((tokens, heads * ROPE), BF),
            jax.ShapeDtypeStruct((2 * heads, keys, HD), BF),
            jax.ShapeDtypeStruct((keys, LAT), F32),
            jax.ShapeDtypeStruct((2, keys, 2 * ROPE), F32),
        ],
        compiler_params=pltpu.CompilerParams(vmem_limit_bytes=32 * 2**20),
    )(live, qn, qr, go, wk, wv, lat, rope2)


def per_device(q_nope, q_rope, latents, w_uk, w_uv, grad_out, prompt_of, live_rows, prompt_block):
    heads = w_uk.shape[0]
    gathered = lax.all_gather(latents, "resp", axis=0, tiled=True)
    rows = gathered.shape[0]
    blocks = prompt_block[prompt_of[0]]
    keys = jnp.take(
        gathered.reshape(rows // P_SIZE, P_SIZE, LAT + ROPE), blocks, axis=0
    ).reshape(-1, LAT + ROPE)
    rope = keys[:, LAT:]
    none = jnp.zeros_like(rope)
    rope2 = jnp.stack(
        [jnp.concatenate([rope, none], axis=1), jnp.concatenate([none, rope], axis=1)]
    )
    d_nope, d_rope, dkv, dc, dr = local_part(
        live_rows[0], q_nope, q_rope, grad_out, w_uk, w_uv, keys[:, :LAT], rope2
    )
    row_of = (blocks[:, None] * P_SIZE + jnp.arange(P_SIZE)[None, :]).reshape(-1)
    select = jnp.arange(rows)[:, None] == row_of[None, :]
    d_keys = jnp.concatenate([dc, dr[0, :, :ROPE] + dr[1, :, ROPE:]], axis=1)
    partial_rows = jnp.dot(select.astype(F32), d_keys, precision=lax.Precision.HIGHEST)
    holder_rows = lax.psum_scatter(partial_rows, "resp", scatter_dimension=0, tiled=True)
    grad_lat = lax.psum(holder_rows, "head")
    spread = jnp.einsum("nk,ukd->und", select.astype(BF), dkv, preferred_element_type=F32)
    summed = lax.psum(spread.astype(BF), "resp").reshape(heads, 2, rows, HD)
    lat_all = gathered[:, :LAT]
    final_uk = jnp.einsum("hnd,nl->hdl", summed[:, 0], lat_all, preferred_element_type=F32)
    final_uv = jnp.einsum("nl,hnd->hld", lat_all, summed[:, 1], preferred_element_type=F32)
    return d_nope, d_rope, grad_lat, final_uk.astype(BF), final_uv.astype(BF)


def solution(mesh):
    in_specs = (
        P("resp", "head"),
        P("resp", "head"),
        P("resp", None),
        P("head", None, None),
        P("head", None, None),
        P("resp", "head"),
        P("resp", None),
        P("resp", None),
        P(),
    )
    out_specs = (
        P("resp", "head"),
        P("resp", "head"),
        P("resp", None),
        P("head", None, None),
        P("head", None, None),
    )
    return jax.shard_map(
        per_device, mesh=mesh, in_specs=in_specs, out_specs=out_specs, check_vma=False
    )
```

time: 300 us -> 201 us (0.67)
  blocking collectives: 188 us -> 16.2 us
  waiting for transfers between devices: 27.5 us -> 133 us
  matrix products: 36.9 us -> 7.17 us
  Pallas kernels: 0 us -> 17.1 us
  local copies, waits for them, and re-layouts: 27 us -> 12 us
  other arithmetic: 5.47 us -> 1.09 us
    psum x1 -> x0, blocking collectives: 171 us -> none  [per_device(): summed = lax.psum((grad_uk, grad_uv), 'resp')]
    psum x0 -> x1, waiting for transfers between devices: none -> 64.7 us  [per_device(): summed = lax.psum(spread.astype(BF), 'resp').reshape(heads, 2, rows, HD)]
    reduce_scatter x1, waiting for transfers between devices: 0.01 us -> 31.9 us  [per_device(): lax.psum_scatter(partial_rows, 'resp', scatter_dimension=0, tiled=True)]
    dot_general x9 -> x4, matrix products: 29.2 us -> 7.17 us  [the longest x1 3.25 us: per_device(): jnp.einsum('hnd,nl->hdl', summed[:, 0], lat_all, preferred_element_type=F32)]
    pallas_call x0 -> x1, Pallas kernels: none -> 17.1 us  [local_part(): pl.pallas_call(local_kernel, grid=(heads // 2,), in_specs=[pl.BlockSpec(m...]
    psum x1, waiting for transfers between devices: 27.4 us -> 36.6 us  [per_device(): grad_lat = lax.psum(holder_rows, 'head')]
    sub x1 -> x0, matrix products: 6.41 us -> none  [per_device(): probs = jax.nn.softmax(scores, axis=-1)]
    reshape x4 -> x1, local copies, waits for them, and re-layouts: 7.78 us -> 1.45 us  [per_device(): summed = lax.psum(spread.astype(BF), 'resp').reshape(heads, 2, rows, HD)]
  transfers between devices with their start and end apart: 2 -> 3, of which waited for: 1 -> 3; matrix products, arithmetic and copies ran while one was open for 8% -> 4% of each run, Pallas kernels for 0% -> 0%
where the time goes in v1:
time: 201 us
  waiting for transfers between devices  133 us (66%)
  Pallas kernels  17.1 us (9%)
  blocking collectives  16.2 us (8%)
  between operations  13.9 us (7%)
  local copies, waits for them, and re-layouts  12 us (6%)
  matrix products  7.17 us (4%)
    psum x1, waiting for transfers between devices, per_device(): summed = lax.psum(spread.astype(BF), 'resp').reshape(heads, 2, rows, HD)  64.7 us
    psum x1, waiting for transfers between devices, per_device(): grad_lat = lax.psum(holder_rows, 'head')  36.6 us
    reduce_scatter x1, waiting for transfers between devices, per_device(): lax.psum_scatter(partial_rows, 'resp', scatter_dimension=0, tiled=True)  31.9 us
    pallas_call x1, Pallas kernels, local_part(): pl.pallas_call(local_kernel, grid=(heads // 2,), in_specs=[pl.BlockSpec(m...  17.1 us
    all_gather x1, blocking collectives, per_device(): gathered = lax.all_gather(latents, 'resp', axis=0, tiled=True)  16.2 us
    unnamed x16, local copies, waits for them, and re-layouts  8.98 us
  transfers between devices with their start and end apart: 3, of which 3 were waited for; matrix products, arithmetic and copies ran while one was open for 4% of the time, Pallas kernels for 0%

profile of v1, /device:TPU:0, one launch (start us, length us, event | category | flops | bytes accessed | tf_op | source)
XLA Modules:
  0.0 200.8 jit_solution(14974227053362819198)
XLA Ops:
  7.2 0.0 copy-start
  7.2 0.0 copy-start.6
  7.2 0.0 copy-start.1
  7.2 0.0 all-reduce.7.cloned.1.call-start
  7.2 0.8 fusion.8
  8.1 0.0 copy-done
  8.1 0.6 gather_fusion
  8.7 0.1 broadcast_in_dim.19
  8.8 0.1 broadcast_in_dim.20
  8.9 16.2 %all_gather.3 = bf16[256,576]{1,0:T(8,128)(2,1)S(1)} all-gather(bf16[32,576]{1,0:T(8,128)(2,1)} %param.11), channel_id=1, replica_groups=mesh['resp'=8,'head'=4] {'resp'}, dimensions={0}, use_global_device_ids=true | all-gather | bytes 331776 | tf_op jit(solution)/shard_map/all_gather | solution.py:124
  25.1 0.6 gather_fusion.1
  25.7 0.1 bitcast_select_fusion
  25.8 0.1 iota_add_fusion
  25.9 0.1 add.67
  26.0 0.1 pad_bitcast_fusion.1
  26.1 0.0 copy-done.6
  26.1 0.0 copy-done.1
  26.1 0.0 copy-start.2
  26.1 1.6 copy-done.2
  27.7 0.0 copy-start.3
  27.7 1.2 copy-done.3
  28.9 0.0 copy-start.4
  28.9 1.2 copy-done.4
  30.2 0.0 copy-start.5
  30.2 1.0 copy-done.5
  31.2 17.1 %shard_map.128 = (bf16[256,2048]{1,0:T(8,128)(2,1)}, bf16[256,1024]{1,0:T(8,128)(2,1)}, bf16[32,128,128]{2,1,0:T(8,128)(2,1)S(1)}, f32[128,512]{1,0:T(8,128)S(1)}, f32[2,128,128]{2,1,0:T(8,128)S(1)}) custom-call(s32[4]{0:T(128)S(1)} %bitcast.37, bf16[256,2048]{1,0:T(8,128)(2,1)S(1)} %copy-done.3, bf16[256,1024]{1,0:T(8,128)(2,1)S(1)} %copy-done.5, ...), custom_call_target="tpu_custom_call" | custom-call | tf_op jit(solution)/shard_map/pallas_call | solution.py:91
  48.3 0.7 convolution_convert_fusion.1
  49.0 1.5 copy.18
  50.5 0.0 all-reduce.7.cloned.1.call-update
  50.5 0.0 reduce-scatter.2.cloned.1.call-start
  50.6 0.1 add_bitcast_fusion
  50.6 1.3 fusion
  51.9 0.0 reduce-scatter.2.cloned.1.call-update
  51.9 0.0 all-reduce.5.cloned.1.call-start
  52.0 64.7 %all-reduce.7.cloned.1.call-done = bf16[16,2,256,128]{2,3,0,1:T(8,128)(2,1)} async-done(((bf16[16,2,256,128]{2,3,0,1:T(8,128)(2,1)}), bf16[16,2,256,128]{2,3,0,1:T(8,128)(2,1)}) %all-reduce.7.cloned.1.call-update) | async-done | bytes 2097168 | tf_op jit(solution)/shard_map/psum | solution.py:145
  116.7 1.9 convert_bitcast_fusion
  118.6 31.9 %reduce-scatter.2.cloned.1.call-done = f32[32,576]{1,0:T(8,128)} async-done(((f32[256,576]{1,0:T(8,128)}), f32[32,576]{1,0:T(8,128)}) %reduce-scatter.2.cloned.1.call-update) | async-done | bytes 73744 | tf_op jit(solution)/shard_map/reduce_scatter | solution.py:142
  150.5 0.0 all-reduce.5.cloned.1.call-update
  150.5 3.2 %convolution_convert_fusion = bf16[16,128,512]{2,1,0:T(8,128)(2,1)} fusion(bf16[16,2,256,128]{2,3,0,1:T(8,128)(2,1)} %all-reduce.7.cloned.1.call-done, bf16[256,576]{1,0:T(8,128)(2,1)S(1)} %all_gather.3), kind=kOutput, calls=%fused_computation.3 | convolution fusion | flops 537919488 | bytes 3407872 | tf_op jit(solution)/shard_map/hnd,nl->hdl/dot_general | solution.py:147
  153.8 2.4 %copy.19 = bf16[16,512,128]{2,1,0:T(8,128)(2,1)} copy(bf16[16,512,128]{1,2,0:T(8,128)(2,1)S(1)} %convert_bitcast_fusion) | data formatting | bytes 4194304
  156.1 36.6 %all-reduce.5.cloned.1.call-done = f32[32,576]{1,0:T(8,128)} async-done(((f32[32,576]{1,0:T(8,128)}), f32[32,576]{1,0:T(8,128)}) %all-reduce.5.cloned.1.call-update) | async-done | bytes 73744 | tf_op jit(solution)/shard_map/psum | solution.py:143
  192.7 1.5 copy.23
  (8 shorter events, 0.1 us)
Async XLA Ops:
  7.2 0.9 copy-start
  7.2 18.9 %copy-start.6 = (s32[1,4]{1,0:T(1,128)S(1)}, s32[1,4]{1,0:T(1,128)}, u32[]{:S(2)}) copy-start(s32[1,4]{1,0:T(1,128)} %param.16) | copy-start | bytes 52
  7.2 18.9 %copy-start.1 = (bf16[16,128,512]{2,1,0:T(8,128)(2,1)S(1)}, bf16[16,128,512]{2,1,0:T(8,128)(2,1)}, u32[]{:S(2)}) copy-start(bf16[16,128,512]{2,1,0:T(8,128)(2,1)} %wk_ref.1) | copy-start | bytes 6291460
  7.2 109.5 %all-reduce.7.cloned.1.call-start = ((), (), s32[]{:S(2)}) async-start(), calls=%async_computation.3 | async-start | bytes 4194304 | tf_op jit(solution)/shard_map/psum | solution.py:145
  26.1 1.6 copy-start.2
  27.7 1.2 copy-start.3
  28.9 1.2 copy-start.4
  30.2 1.0 copy-start.5
  50.5 100.0 %reduce-scatter.2.cloned.1.call-start = ((), (), s32[]{:S(2)}) async-start(), calls=%async_computation.1 | async-start | bytes 737280 | tf_op jit(solution)/shard_map/reduce_scatter | solution.py:142
  51.9 140.8 %all-reduce.5.cloned.1.call-start = ((), (), s32[]{:S(2)}) async-start(), calls=%async_computation.2 | async-start | bytes 163840 | tf_op jit(solution)/shard_map/psum | solution.py:143
Sparse Core Ops, SparseCore 0:
  50.6 66.0 all-reduce.6
  119.5 30.9 reduce-scatter.1
  153.4 39.2 all-reduce.4

commit v2 on v1

--- a/solution.py
+++ b/solution.py
@@ -75,8 +75,8 @@
         dqr = dqr + dot_nn(ds, rope)
         dk = (dot_tn(ds, qn) * SCALE).astype(BF)
         dv = dot_tn(pb, g).astype(BF)
-        dkv_ref[2 * i] = dk
-        dkv_ref[2 * i + 1] = dv
+        dkv_ref[0, :, 2 * i * HD:(2 * i + 1) * HD] = dk
+        dkv_ref[0, :, (2 * i + 1) * HD:(2 * i + 2) * HD] = dv
         dc = dc + dot_nn(dk, wk_ref[i]) + dot_nt(dv, wv_ref[i])
         dr_ref[i] += dot_tn(ds, qr) * SCALE
     dqr_ref[...] = (dqr * SCALE).astype(BF)
@@ -104,14 +104,14 @@
         out_specs=[
             pl.BlockSpec((tokens, 2 * HD), lambda i: (0, i)),
             pl.BlockSpec((tokens, 2 * ROPE), lambda i: (0, i)),
-            pl.BlockSpec((4, keys, HD), lambda i: (i, 0, 0)),
+            pl.BlockSpec((1, keys, 4 * HD), lambda i: (i, 0, 0)),
             full(keys, LAT),
             full(2, keys, 2 * ROPE),
         ],
         out_shape=[
             jax.ShapeDtypeStruct((tokens, heads * HD), BF),
             jax.ShapeDtypeStruct((tokens, heads * ROPE), BF),
-            jax.ShapeDtypeStruct((2 * heads, keys, HD), BF),
+            jax.ShapeDtypeStruct((heads // 2, keys, 4 * HD), BF),
             jax.ShapeDtypeStruct((keys, LAT), F32),
             jax.ShapeDtypeStruct((2, keys, 2 * ROPE), F32),
         ],
@@ -119,13 +119,263 @@
     )(live, qn, qr, go, wk, wv, lat, rope2)
 
 
-def per_device(q_nope, q_rope, latents, w_uk, w_uv, grad_out, prompt_of, live_rows, prompt_block):
-    heads = w_uk.shape[0]
-    gathered = lax.all_gather(latents, "resp", axis=0, tiled=True)
-    rows = gathered.shape[0]
+MESH = pl.DeviceIdType.MESH
+ID_ROWS = 16
+
+
+def at_resp(r):
+    return (r, lax.axis_index("head"))
+
+
+def greet(peers):
+    barrier = pltpu.get_barrier_semaphore()
+    for peer in peers:
+        pl.semaphore_signal(barrier, inc=1, device_id=peer, device_id_type=MESH)
+    pl.semaphore_wait(barrier, len(peers))
+
+
+def spread_blocks(n, me, buf, send, near, far, passed):
+    sibling = me + 1 - 2 * lax.rem(me, 2)
+
+    def copy(slot, to, s, recv):
+        return pltpu.make_async_remote_copy(
+            src_ref=buf.at[slot], dst_ref=buf.at[slot], send_sem=send.at[s], recv_sem=recv,
+            device_id=at_resp(to), device_id_type=MESH,
+        )
+
+    hops = n // 2
+    out = [copy(me, lax.rem(me + 2 * k, n), k, far.at[k]) for k in range(1, hops)]
+    own = copy(me, sibling, 0, near.at[0])
+    for c in out:
+        c.start()
+    own.start()
+    handed = []
+    for k in range(1, hops):
+        out[k - 1].wait_recv()
+        c = copy(lax.rem(me - 2 * k + n, n), sibling, hops + k - 1, passed.at[k])
+        c.start()
+        handed.append(c)
+    own.wait()
+    for c in out:
+        c.wait_send()
+    for c in handed:
+        c.wait()
+
+
+def gather_kernel(n, mine_ref, all_ref, send, near, far, passed):
+    me = lax.axis_index("resp")
+    sibling = me + 1 - 2 * lax.rem(me, 2)
+    greet([at_resp(lax.rem(me + 2 * k, n)) for k in range(1, n // 2)] + [at_resp(sibling)])
+    all_ref[me] = mine_ref[...]
+    spread_blocks(n, me, all_ref, send, near, far, passed)
+
+
+def spread_scratch(n):
+    return [
+        pltpu.SemaphoreType.DMA((n,)),
+        pltpu.SemaphoreType.DMA((1,)),
+        pltpu.SemaphoreType.DMA((n // 2,)),
+        pltpu.SemaphoreType.DMA((n // 2,)),
+    ]
+
+
+VM = pl.BlockSpec(memory_space=pltpu.VMEM)
+
+
+def gather_blocks(n, mine):
+    return pl.pallas_call(
+        functools.partial(gather_kernel, n),
+        out_shape=jax.ShapeDtypeStruct((n,) + mine.shape, mine.dtype),
+        in_specs=[VM],
+        out_specs=VM,
+        scratch_shapes=spread_scratch(n),
+        compiler_params=pltpu.CompilerParams(
+            collective_id=1, has_side_effects=True, vmem_limit_bytes=6 * 2**20
+        ),
+    )(mine)
+
+
+CHIPS = 4
+PARTS = 8
+
+
+def sum_kernel(
+    n, nh, dkv_ref, rows_ref, sel_ref, all_ref, lat_ref,
+    got_rows, at_head, sib, mine, outer, half, other,
+    s2, r2, s3, r3, ss, sr, es, er, hs, hr, ts, tr, gs, gr,
+):
+    me = lax.axis_index("resp")
+    head = lax.axis_index("head")
+    core = lax.rem(me, 2)
+    z = me // 2
+    sibling = me + 1 - 2 * core
+    beside = 2 * (z + 1 - 2 * lax.rem(z, 2)) + core
+    across = 2 * (CHIPS - 1 - z) + core
+    inner = (z == 1) | (z == 2)
+    peers = [lax.rem(me + k, n) for k in range(1, n)]
+    heads = [lax.rem(head + k, nh) for k in range(1, nh)]
+    greet([at_resp(r) for r in peers] + [(me, h) for h in heads])
+    pairs = dkv_ref.shape[0] // 2
+    keys = mine.shape[1]
+
+    def copy(src, dst, s, r, i, to):
+        return pltpu.make_async_remote_copy(
+            src_ref=src, dst_ref=dst, send_sem=s.at[i], recv_sem=r.at[i],
+            device_id=to, device_id_type=MESH,
+        )
+
+    sib_copies = [
+        copy(dkv_ref.at[(1 - core) * pairs + j], sib.at[j], ss, sr, j, at_resp(sibling))
+        for j in range(pairs)
+    ]
+    for c in sib_copies:
+        c.start()
+    row_copies = [
+        copy(rows_ref.at[peers[k]], got_rows.at[k], s2, r2, k, at_resp(peers[k])) for k in range(n - 1)
+    ]
+    for c in row_copies:
+        c.start()
+    head_copies = [
+        copy(at_head.at[head], at_head.at[head], s3, r3, k, (me, heads[k])) for k in range(nh - 1)
+    ]
+    inwards = [copy(mine.at[i], outer.at[i], es, er, i, at_resp(beside)) for i in range(PARTS)]
+    middle = [copy(half.at[i], other.at[i], hs, hr, i, at_resp(across)) for i in range(PARTS)]
+    slots = [all_ref.at[core * PARTS + i] for i in range(PARTS)]
+    outwards = [copy(slots[i], slots[i], ts, tr, i, at_resp(beside)) for i in range(PARTS)]
+    shared = [copy(slots[i], slots[i], gs, gr, i, at_resp(sibling)) for i in range(PARTS)]
+
+    def chip_terms(j):
+        sib_copies[j].wait_recv()
+        total = dot_nn(sel_ref[me], dkv_ref[core * pairs + j]) + dot_nn(sel_ref[sibling], sib[j])
+        mine[2 * j] = total[:keys].astype(BF)
+        mine[2 * j + 1] = total[keys:].astype(BF)
+
+    def sum_rows():
+        rows = rows_ref[me].astype(F32)
+        for k in range(n - 1):
+            row_copies[k].wait_recv()
+            rows = rows + got_rows[k].astype(F32)
+        at_head[head] = rows
+        for c in head_copies:
+            c.start()
+
+    def finish(i):
+        middle[i].wait_recv()
+        all_ref[core * PARTS + i] = (half[i].astype(F32) + other[i].astype(F32)).astype(BF)
+        outwards[i].start()
+        shared[i].start()
+
+    @pl.when(inner)
+    def _():
+        for j in range(pairs):
+            chip_terms(j)
+        for i in range(PARTS):
+            inwards[i].wait_recv()
+            half[i] = (mine[i].astype(F32) + outer[i].astype(F32)).astype(BF)
+            middle[i].start()
+            if i >= 1:
+                finish(i - 1)
+            if i == PARTS // 2:
+                sum_rows()
+        finish(PARTS - 1)
+        for i in range(PARTS):
+            middle[i].wait_send()
+            outwards[i].wait_send()
+
+    @pl.when(jnp.logical_not(inner))
+    def _():
+        for j in range(pairs):
+            chip_terms(j)
+            inwards[2 * j].start()
+            inwards[2 * j + 1].start()
+        sum_rows()
+        for i in range(PARTS):
+            outwards[i].wait_recv()
+            shared[i].start()
+        for i in range(PARTS):
+            inwards[i].wait_send()
+
+    for c in head_copies:
+        c.wait()
+    lat = at_head[0]
+    for h in range(1, nh):
+        lat = lat + at_head[h]
+    lat_ref[...] = lat
+    for c in shared:
+        c.wait()
+    for c in row_copies + sib_copies:
+        c.wait_send()
+
+
+def sum_parts(n, nh, dkv, rows, select):
+    pairs, keys, wide = dkv.shape
+    dma = lambda k: pltpu.SemaphoreType.DMA((k,))
+    part = pltpu.VMEM((PARTS, select.shape[1] // 2, wide), BF)
+    summed, lat = pl.pallas_call(
+        functools.partial(sum_kernel, n, nh),
+        out_shape=[
+            jax.ShapeDtypeStruct((2 * pairs, select.shape[1] // 2, wide), BF),
+            jax.ShapeDtypeStruct(rows.shape[1:], F32),
+        ],
+        in_specs=[VM] * 3,
+        out_specs=[VM] * 2,
+        scratch_shapes=[
+            pltpu.VMEM((n - 1,) + rows.shape[1:], BF),
+            pltpu.VMEM((nh,) + rows.shape[1:], F32),
+            pltpu.VMEM((pairs // 2, keys, wide), BF),
+            part, part, part, part,
+            dma(n - 1), dma(n - 1), dma(nh - 1), dma(nh - 1), dma(pairs // 2), dma(pairs // 2),
+        ] + [dma(PARTS)] * 8,
+        compiler_params=pltpu.CompilerParams(
+            collective_id=2, has_side_effects=True, vmem_limit_bytes=32 * 2**20
+        ),
+    )(dkv, rows, select)
+    return summed.reshape(pairs, select.shape[1], wide), lat
+
+
+def weights_kernel(sum_ref, lat_ref, duk_ref, duv_ref):
+    lat = lat_ref[...]
+    for i in range(2):
+        at = 2 * i * HD
+        duk_ref[i] = dot_tn(sum_ref[0, :, at:at + HD], lat).astype(BF)
+        duv_ref[i] = dot_tn(lat, sum_ref[0, :, at + HD:at + 2 * HD]).astype(BF)
+
+
+def weight_grads(summed, lat_all):
+    pairs, rows, wide = summed.shape
+    return pl.pallas_call(
+        weights_kernel,
+        grid=(pairs,),
+        in_specs=[
+            pl.BlockSpec((1, rows, wide), lambda i: (i, 0, 0)),
+            pl.BlockSpec((rows, LAT), lambda i: (0, 0)),
+        ],
+        out_specs=[
+            pl.BlockSpec((2, HD, LAT), lambda i: (i, 0, 0)),
+            pl.BlockSpec((2, LAT, HD), lambda i: (i, 0, 0)),
+        ],
+        out_shape=[
+            jax.ShapeDtypeStruct((2 * pairs, HD, LAT), BF),
+            jax.ShapeDtypeStruct((2 * pairs, LAT, HD), BF),
+        ],
+        compiler_params=pltpu.CompilerParams(vmem_limit_bytes=32 * 2**20),
+    )(summed, lat_all)
+
+
+def per_device(
+    n, nh, q_nope, q_rope, latents, w_uk, w_uv, grad_out, prompt_of, live_rows, prompt_block
+):
+    pairs = w_uk.shape[0] // 2
+    held = latents.shape[0]
+    stretches = prompt_of.shape[1]
     blocks = prompt_block[prompt_of[0]]
+    ids = jnp.zeros((ID_ROWS, LAT + ROPE), BF).at[0, :stretches].set(blocks.astype(BF))
+    gathered = gather_blocks(n, jnp.concatenate([latents, ids], axis=0))
+    table = gathered[:, :held].reshape(n * held, LAT + ROPE)
+    all_blocks = gathered[:, held, :stretches].astype(jnp.int32)
+    rows = n * held
     keys = jnp.take(
-        gathered.reshape(rows // P_SIZE, P_SIZE, LAT + ROPE), blocks, axis=0
+        table.reshape(rows // P_SIZE, P_SIZE, LAT + ROPE), blocks, axis=0
     ).reshape(-1, LAT + ROPE)
     rope = keys[:, LAT:]
     none = jnp.zeros_like(rope)
@@ -135,18 +385,27 @@
     d_nope, d_rope, dkv, dc, dr = local_part(
         live_rows[0], q_nope, q_rope, grad_out, w_uk, w_uv, keys[:, :LAT], rope2
     )
-    row_of = (blocks[:, None] * P_SIZE + jnp.arange(P_SIZE)[None, :]).reshape(-1)
-    select = jnp.arange(rows)[:, None] == row_of[None, :]
+
+    def rows_of(which):
+        at = which[..., :, None] * P_SIZE + jnp.arange(P_SIZE)
+        at = at.reshape(which.shape[:-1] + (-1,))
+        return jnp.arange(rows)[:, None] == at[..., None, :]
+
     d_keys = jnp.concatenate([dc, dr[0, :, :ROPE] + dr[1, :, ROPE:]], axis=1)
+    select = rows_of(blocks)
     partial_rows = jnp.dot(select.astype(F32), d_keys, precision=lax.Precision.HIGHEST)
-    holder_rows = lax.psum_scatter(partial_rows, "resp", scatter_dimension=0, tiled=True)
-    grad_lat = lax.psum(holder_rows, "head")
-    spread = jnp.einsum("nk,ukd->und", select.astype(BF), dkv, preferred_element_type=F32)
-    summed = lax.psum(spread.astype(BF), "resp").reshape(heads, 2, rows, HD)
-    lat_all = gathered[:, :LAT]
-    final_uk = jnp.einsum("hnd,nl->hdl", summed[:, 0], lat_all, preferred_element_type=F32)
-    final_uv = jnp.einsum("nl,hnd->hld", lat_all, summed[:, 1], preferred_element_type=F32)
-    return d_nope, d_rope, grad_lat, final_uk.astype(BF), final_uv.astype(BF)
+    if pairs == n == 2 * CHIPS:
+        summed, grad_lat = sum_parts(
+            n, nh, dkv, partial_rows.astype(BF).reshape(n, held, LAT + ROPE),
+            rows_of(all_blocks).astype(BF),
+        )
+    else:
+        holder_rows = lax.psum_scatter(partial_rows, "resp", scatter_dimension=0, tiled=True)
+        grad_lat = lax.psum(holder_rows, "head")
+        spread = jnp.einsum("nk,ukd->und", select.astype(BF), dkv, preferred_element_type=F32)
+        summed = lax.psum(spread, "resp").astype(BF)
+    final_uk, final_uv = weight_grads(summed, table[:, :LAT])
+    return d_nope, d_rope, grad_lat, final_uk, final_uv
 
 
 def solution(mesh):
@@ -169,5 +428,5 @@
         P("head", None, None),
     )
     return jax.shard_map(
-        per_device, mesh=mesh, in_specs=in_specs, out_specs=out_specs, check_vma=False
+        functools.partial(per_device, mesh.shape["resp"], mesh.shape["head"]), mesh=mesh, in_specs=in_specs, out_specs=out_specs, check_vma=False
     )

time: 201 us -> 89.4 us (0.44)
  waiting for transfers between devices: 133 us -> 0 us
  Pallas kernels: 17.1 us -> 77.8 us
  blocking collectives: 16.2 us -> 0 us
  between operations: 13.9 us -> 0.81 us
  matrix products: 7.17 us -> 0.46 us
  local copies, waits for them, and re-layouts: 12 us -> 8.27 us
    psum x2 -> x0, waiting for transfers between devices: 101 us -> none  [the longest x1 64.7 us: per_device(): summed = lax.psum(spread.astype(BF), 'resp').reshape(heads, 2, rows, HD)]
    pallas_call x0 -> x3, Pallas kernels: none -> 60.7 us  [the longest x1 44.1 us: sum_parts(): pl.pallas_call(functools.partial(sum_kernel, n, nh), out_shape=[jax.Shape...]
    reduce_scatter x1 -> x0, waiting for transfers between devices: 31.9 us -> none  [per_device(): lax.psum_scatter(partial_rows, 'resp', scatter_dimension=0, tiled=True)]
    all_gather x1 -> x0, blocking collectives: 16.2 us -> none  [per_device(): gathered = lax.all_gather(latents, 'resp', axis=0, tiled=True)]
    dot_general x3 -> x0, matrix products: 5.91 us -> none  [the longest x1 3.25 us: per_device(): jnp.einsum('hnd,nl->hdl', summed[:, 0], lat_all, preferred_element_type=F32)]
    unnamed x16 -> x19, local copies, waits for them, and re-layouts: 8.98 us -> 6.14 us
  transfers between devices with their start and end apart: 3 -> 0, of which waited for: 3 -> 0; matrix products, arithmetic and copies ran while one was open for 4% -> 0% of each run, Pallas kernels for 0% -> 0%
where the time goes in v2:
time: 89.4 us; the launch traced here: 89.1 us
  Pallas kernels  77.8 us (87%)
  local copies, waits for them, and re-layouts  8.27 us (9%)
  other arithmetic  1.8 us (2%)
    pallas_call x1, Pallas kernels, sum_parts(): pl.pallas_call(functools.partial(sum_kernel, n, nh), out_shape=[jax.Shape...  44.1 us
    pallas_call x1, Pallas kernels, local_part(): pl.pallas_call(local_kernel, grid=(heads // 2,), in_specs=[pl.BlockSpec(m...  17.1 us
    pallas_call x1, Pallas kernels, gather_blocks(): pl.pallas_call(functools.partial(gather_kernel, n), out_shape=jax.ShapeDt...  11.7 us
    unnamed x19, local copies, waits for them, and re-layouts  6.14 us
    pallas_call x1, Pallas kernels, weight_grads(): pl.pallas_call(weights_kernel, grid=(pairs,), in_specs=[pl.BlockSpec((1,...  4.94 us

profile of v2, /device:TPU:0, one launch (start us, length us, event | category | flops | bytes accessed | tf_op | source)
XLA Modules:
  0.0 89.1 jit_solution(15376573303004339753)
XLA Ops:
  0.6 0.0 copy-start
  0.6 0.7 fusion.7
  1.3 0.1 add.89
  1.4 0.0 copy-done
  1.4 0.0 copy-start.1
  1.4 0.0 copy-start.7
  1.4 0.0 copy-start.8
  1.4 0.6 gather_fusion
  2.1 0.1 broadcast_in_dim.22
  2.2 0.1 broadcast_in_dim.23
  2.3 0.1 add.86
  2.3 0.1 add.87
  2.4 0.8 fusion.6.mine_ref
  3.2 11.7 %shard_map.128 = bf16[8,48,576]{2,1,0:T(8,128)(2,1)S(1)} custom-call(bf16[48,576]{1,0:T(8,128)(2,1)S(1)} %fusion.6.mine_ref), custom_call_target="tpu_custom_call" | custom-call | tf_op jit(solution)/shard_map/pallas_call | solution.py:186
  15.0 0.1 add.93
  15.0 0.1 add.94
  15.1 0.6 gather_fusion.1
  15.7 0.1 bitcast_select_fusion
  15.8 0.1 pad_bitcast_fusion.1
  16.0 0.1 fusion.sel_ref
  16.1 0.0 copy-done.1
  16.1 0.0 copy-done.7
  16.1 0.0 copy-done.8
  16.1 0.0 copy-start.2
  16.1 1.6 %copy-done.2 = bf16[16,512,128]{2,1,0:T(8,128)(2,1)S(1)} copy-done((bf16[16,512,128]{2,1,0:T(8,128)(2,1)S(1)}, bf16[16,512,128]{2,1,0:T(8,128)(2,1)}, u32[]{:S(2)}) %copy-start.2) | copy-done | bytes 2097176
  17.7 0.0 copy-start.5
  17.7 1.2 %copy-done.5 = bf16[256,2048]{1,0:T(8,128)(2,1)S(1)} copy-done((bf16[256,2048]{1,0:T(8,128)(2,1)S(1)}, bf16[256,2048]{1,0:T(8,128)(2,1)}, u32[]{:S(2)}) %copy-start.5) | copy-done | bytes 1048600
  18.9 0.0 copy-start.6
  18.9 1.2 %copy-done.6 = bf16[256,2048]{1,0:T(8,128)(2,1)S(1)} copy-done((bf16[256,2048]{1,0:T(8,128)(2,1)S(1)}, bf16[256,2048]{1,0:T(8,128)(2,1)}, u32[]{:S(2)}) %copy-start.6) | copy-done | bytes 1048600
  20.2 17.1 %shard_map.129 = (bf16[256,2048]{1,0:T(8,128)(2,1)}, bf16[256,1024]{1,0:T(8,128)(2,1)}, bf16[8,128,512]{2,1,0:T(8,128)(2,1)S(1)}, f32[128,512]{1,0:T(8,128)S(1)}, f32[2,128,128]{2,1,0:T(8,128)S(1)}) custom-call(s32[4]{0:T(128)S(1)} %bitcast.25, bf16[256,2048]{1,0:T(8,128)(2,1)S(1)} %copy-done.5, bf16[256,1024]{1,0:T(8,128)(2,1)S(1)} %copy-done.7, ...), custom_call_target="tpu_custom_call" | custom-call | tf_op jit(solution)/shard_map/pallas_call | solution.py:91
  37.3 0.0 copy-start.3
  37.3 1.0 %copy-done.3 = bf16[8,128,512]{2,1,0:T(8,128)(2,1)} copy-done((bf16[8,128,512]{2,1,0:T(8,128)(2,1)}, bf16[8,128,512]{2,1,0:T(8,128)(2,1)S(1)}, u32[]{:S(2)}) %copy-start.3) | copy-done | bytes 1048600
  38.2 0.0 copy-start.4
  38.2 0.1 add_bitcast_fusion
  38.3 0.5 convolution_convert_fusion
  38.8 0.2 copy.20
  39.0 0.5 copy-done.4
  39.5 44.1 %shard_map.130 = (bf16[16,128,512]{2,1,0:T(8,128)(2,1)S(1)}, f32[32,576]{1,0:T(8,128)S(1)}) custom-call(bf16[8,128,512]{2,1,0:T(8,128)(2,1)S(1)} %copy-done.4, bf16[8,32,576]{2,1,0:T(8,128)(2,1)S(1)} %bitcast.24, bf16[8,256,128]{2,1,0:T(8,128)(2,1)S(1)} %fusion.sel_ref), custom_call_target="tpu_custom_call" | custom-call | tf_op jit(solution)/shard_map/pallas_call | solution.py:314
  83.5 4.9 %shard_map.131 = (bf16[16,128,512]{2,1,0:T(8,128)(2,1)}, bf16[16,512,128]{2,1,0:T(8,128)(2,1)}) custom-call(bf16[8,256,512]{2,1,0:T(8,128)(2,1)S(1)} %bitcast.23, bf16[256,512]{1,0:T(8,128)(2,1)S(1)} %slice.50.lat_ref), custom_call_target="tpu_custom_call" | custom-call | tf_op jit(solution)/shard_map/pallas_call | solution.py:346
  88.5 0.6 copy.25
  (14 shorter events, 0.1 us)
Async XLA Ops:
  0.6 0.8 copy-start
  1.4 14.7 %copy-start.1 = (bf16[16,128,512]{2,1,0:T(8,128)(2,1)S(1)}, bf16[16,128,512]{2,1,0:T(8,128)(2,1)}, u32[]{:S(2)}) copy-start(bf16[16,128,512]{2,1,0:T(8,128)(2,1)} %wk_ref.1) | copy-start | bytes 6291460
  1.4 14.7 %copy-start.7 = (bf16[256,1024]{1,0:T(8,128)(2,1)S(1)}, bf16[256,1024]{1,0:T(8,128)(2,1)}, u32[]{:S(2)}) copy-start(bf16[256,1024]{1,0:T(8,128)(2,1)} %qr_ref.1) | copy-start | bytes 1572868
  1.4 14.7 %copy-start.8 = (s32[1,4]{1,0:T(1,128)S(1)}, s32[1,4]{1,0:T(1,128)}, u32[]{:S(2)}) copy-start(s32[1,4]{1,0:T(1,128)} %param.18) | copy-start | bytes 52
  16.1 1.6 %copy-start.2 = (bf16[16,512,128]{2,1,0:T(8,128)(2,1)S(1)}, bf16[16,512,128]{2,1,0:T(8,128)(2,1)}, u32[]{:S(2)}) copy-start(bf16[16,512,128]{2,1,0:T(8,128)(2,1)} %wv_ref.1) | copy-start | bytes 6291460
  17.7 1.2 %copy-start.5 = (bf16[256,2048]{1,0:T(8,128)(2,1)S(1)}, bf16[256,2048]{1,0:T(8,128)(2,1)}, u32[]{:S(2)}) copy-start(bf16[256,2048]{1,0:T(8,128)(2,1)} %qn_ref.1) | copy-start | bytes 3145732
  18.9 1.2 %copy-start.6 = (bf16[256,2048]{1,0:T(8,128)(2,1)S(1)}, bf16[256,2048]{1,0:T(8,128)(2,1)}, u32[]{:S(2)}) copy-start(bf16[256,2048]{1,0:T(8,128)(2,1)} %go_ref.1) | copy-start | bytes 3145732
  37.3 1.0 %copy-start.3 = (bf16[8,128,512]{2,1,0:T(8,128)(2,1)}, bf16[8,128,512]{2,1,0:T(8,128)(2,1)S(1)}, u32[]{:S(2)}) copy-start(bf16[8,128,512]{2,1,0:T(8,128)(2,1)S(1)} %get-tuple-element.28.dkv_ref) | copy-start | bytes 3145732
  38.2 1.2 %copy-start.4 = (bf16[8,128,512]{2,1,0:T(8,128)(2,1)S(1)}, bf16[8,128,512]{2,1,0:T(8,128)(2,1)}, u32[]{:S(2)}) copy-start(bf16[8,128,512]{2,1,0:T(8,128)(2,1)} %copy-done.3) | copy-start | bytes 3145732

commit v3 on v2

--- a/solution.py
+++ b/solution.py
@@ -15,6 +15,7 @@
 SCALE = (HD + ROPE) ** (-0.5)
 BF = jnp.bfloat16
 F32 = jnp.float32
+STEP = 4
 
 
 def dot_nn(a, b):
@@ -30,11 +31,11 @@
 
 
 def local_kernel(
-    live_ref, qn_ref, qr_ref, go_ref, wk_ref, wv_ref, lat_ref, rope_ref,
-    dqn_ref, dqr_ref, dkv_ref, dc_ref, dr_ref,
+    live_ref, qn_ref, qr_ref, go_ref, wk_ref, wv_ref, keys_ref,
+    dqn_ref, dqr_ref, dkv_ref, dkeys_ref, dc_ref, dr_ref,
 ):
     tokens = qn_ref.shape[0]
-    keys = lat_ref.shape[0]
+    keys = keys_ref.shape[0]
     stretches = keys // P_SIZE
     row = lax.broadcasted_iota(jnp.int32, (tokens, keys), 0)
     lane = lax.broadcasted_iota(jnp.int32, (tokens, keys), 1)
@@ -44,9 +45,10 @@
     for c in range(stretches):
         limit = jnp.where(row_h // ROWS == c, live_ref[c], limit)
     live = (row_h % ROWS) < limit
-    lat = lat_ref[...]
-    qr = qr_ref[...]
-    dqr = jnp.zeros((tokens, 2 * ROPE), F32)
+    lat = keys_ref[:, :LAT]
+    rope = keys_ref[:, LAT:]
+    none = jnp.zeros_like(rope)
+    ropes = [jnp.concatenate([rope, none], axis=1), jnp.concatenate([none, rope], axis=1)]
     dc = jnp.zeros((keys, LAT), F32)
 
     @pl.when(pl.program_id(0) == 0)
@@ -54,69 +56,75 @@
         dc_ref[...] = jnp.zeros_like(dc_ref)
         dr_ref[...] = jnp.zeros_like(dr_ref)
 
-    for i in range(2):
-        cols = slice(i * HD, (i + 1) * HD)
-        qn = qn_ref[:, cols]
-        g = jnp.where(live, go_ref[:, cols], jnp.zeros((), BF))
-        kn = dot_nt(lat, wk_ref[i]).astype(BF)
-        vn = dot_nn(lat, wv_ref[i]).astype(BF)
-        rope = rope_ref[i]
-        s = dot_nt(
-            jnp.concatenate([qn, qr], axis=1), jnp.concatenate([kn, rope], axis=1)
-        ) * SCALE
-        s = jnp.where(own, s, -jnp.inf)
-        e = jnp.exp(s - jnp.max(s, axis=1, keepdims=True))
-        p = e / jnp.sum(e, axis=1, keepdims=True)
-        pb = p.astype(BF)
-        dp = dot_nt(g, vn)
-        delta = jnp.sum(p * dp, axis=1, keepdims=True)
-        ds = (p * (dp - delta)).astype(BF)
-        dqn_ref[:, cols] = (dot_nn(ds, kn) * SCALE).astype(BF)
-        dqr = dqr + dot_nn(ds, rope)
-        dk = (dot_tn(ds, qn) * SCALE).astype(BF)
-        dv = dot_tn(pb, g).astype(BF)
-        dkv_ref[0, :, 2 * i * HD:(2 * i + 1) * HD] = dk
-        dkv_ref[0, :, (2 * i + 1) * HD:(2 * i + 2) * HD] = dv
-        dc = dc + dot_nn(dk, wk_ref[i]) + dot_nt(dv, wv_ref[i])
-        dr_ref[i] += dot_tn(ds, qr) * SCALE
-    dqr_ref[...] = (dqr * SCALE).astype(BF)
+    for pair in range(STEP // 2):
+        rope_cols = slice(2 * pair * ROPE, 2 * (pair + 1) * ROPE)
+        qr = qr_ref[:, rope_cols]
+        dqr = jnp.zeros((tokens, 2 * ROPE), F32)
+        for i in range(2):
+            at = 2 * pair + i
+            cols = slice(at * HD, (at + 1) * HD)
+            g = jnp.where(live, go_ref[:, cols], jnp.zeros((), BF))
+            kn = dot_nt(lat, wk_ref[at]).astype(BF)
+            vn = dot_nn(lat, wv_ref[at]).astype(BF)
+            q_all = jnp.concatenate([qn_ref[:, cols], qr], axis=1)
+            k_all = jnp.concatenate([kn, ropes[i]], axis=1)
+            s = jnp.where(own, dot_nt(q_all, k_all) * SCALE, -jnp.inf)
+            e = jnp.exp(s - jnp.max(s, axis=1, keepdims=True))
+            p = e * (1.0 / jnp.sum(e, axis=1, keepdims=True))
+            dp = dot_nt(g, vn)
+            delta = jnp.sum(p * dp, axis=1, keepdims=True)
+            ds = (p * (dp - delta)).astype(BF)
+            dq = dot_nn(ds, k_all) * SCALE
+            dqn_ref[:, cols] = dq[:, :HD].astype(BF)
+            dqr = dqr + dq[:, HD:]
+            dk_all = dot_tn(ds, q_all) * SCALE
+            dk = dk_all[:, :HD].astype(BF)
+            dv = dot_tn(p.astype(BF), g).astype(BF)
+            dkv_ref[pair, :, 2 * i * HD:(2 * i + 1) * HD] = dk
+            dkv_ref[pair, :, (2 * i + 1) * HD:(2 * i + 2) * HD] = dv
+            dc = dc + dot_nn(dk, wk_ref[at]) + dot_nt(dv, wv_ref[at])
+            dr_ref[i] += dk_all[:, HD:]
+        dqr_ref[:, rope_cols] = dqr.astype(BF)
     dc_ref[...] += dc
 
-
-def local_part(live, qn, qr, go, wk, wv, lat, rope2):
+    @pl.when(pl.program_id(0) == pl.num_programs(0) - 1)
+    def _():
+        dkeys_ref[:, :LAT] = dc_ref[...]
+        dkeys_ref[:, LAT:] = dr_ref[0][:, :ROPE] + dr_ref[1][:, ROPE:]
+
+
+def local_part(live, qn, qr, go, wk, wv, k_rows):
     heads = wk.shape[0]
     tokens = qn.shape[0]
-    keys = lat.shape[0]
+    keys = k_rows.shape[0]
     full = lambda *shape: pl.BlockSpec(shape, lambda i: (0,) * len(shape))
     return pl.pallas_call(
         local_kernel,
-        grid=(heads // 2,),
+        grid=(heads // STEP,),
         in_specs=[
             pl.BlockSpec(memory_space=pltpu.SMEM),
-            pl.BlockSpec((tokens, 2 * HD), lambda i: (0, i)),
-            pl.BlockSpec((tokens, 2 * ROPE), lambda i: (0, i)),
-            pl.BlockSpec((tokens, 2 * HD), lambda i: (0, i)),
-            pl.BlockSpec((2, HD, LAT), lambda i: (i, 0, 0)),
-            pl.BlockSpec((2, LAT, HD), lambda i: (i, 0, 0)),
-            full(keys, LAT),
-            full(2, keys, 2 * ROPE),
+            pl.BlockSpec((tokens, STEP * HD), lambda i: (0, i)),
+            pl.BlockSpec((tokens, STEP * ROPE), lambda i: (0, i)),
+            pl.BlockSpec((tokens, STEP * HD), lambda i: (0, i)),
+            pl.BlockSpec((STEP, HD, LAT), lambda i: (i, 0, 0)),
+            pl.BlockSpec((STEP, LAT, HD), lambda i: (i, 0, 0)),
+            full(keys, LAT + ROPE),
         ],
         out_specs=[
-            pl.BlockSpec((tokens, 2 * HD), lambda i: (0, i)),
-            pl.BlockSpec((tokens, 2 * ROPE), lambda i: (0, i)),
-            pl.BlockSpec((1, keys, 4 * HD), lambda i: (i, 0, 0)),
-            full(keys, LAT),
-            full(2, keys, 2 * ROPE),
+            pl.BlockSpec((tokens, STEP * HD), lambda i: (0, i)),
+            pl.BlockSpec((tokens, STEP * ROPE), lambda i: (0, i)),
+            pl.BlockSpec((STEP // 2, keys, 4 * HD), lambda i: (i, 0, 0)),
+            full(keys, LAT + ROPE),
         ],
         out_shape=[
             jax.ShapeDtypeStruct((tokens, heads * HD), BF),
             jax.ShapeDtypeStruct((tokens, heads * ROPE), BF),
             jax.ShapeDtypeStruct((heads // 2, keys, 4 * HD), BF),
-            jax.ShapeDtypeStruct((keys, LAT), F32),
-            jax.ShapeDtypeStruct((2, keys, 2 * ROPE), F32),
-        ],
-        compiler_params=pltpu.CompilerParams(vmem_limit_bytes=32 * 2**20),
-    )(live, qn, qr, go, wk, wv, lat, rope2)
+            jax.ShapeDtypeStruct((keys, LAT + ROPE), F32),
+        ],
+        scratch_shapes=[pltpu.VMEM((keys, LAT), F32), pltpu.VMEM((2, keys, 2 * ROPE), F32)],
+        compiler_params=pltpu.CompilerParams(vmem_limit_bytes=60 * 2**20),
+    )(live, qn, qr, go, wk, wv, k_rows)
 
 
 MESH = pl.DeviceIdType.MESH
@@ -333,31 +341,39 @@
     return summed.reshape(pairs, select.shape[1], wide), lat
 
 
-def weights_kernel(sum_ref, lat_ref, duk_ref, duv_ref):
+def weights_kernel(sum_ref, lat_ref, duk_ref, duv_ref, lat_t):
+    @pl.when(pl.program_id(0) == 0)
+    def _():
+        lat_t[...] = lat_ref[...].T
+
     lat = lat_ref[...]
-    for i in range(2):
-        at = 2 * i * HD
-        duk_ref[i] = dot_tn(sum_ref[0, :, at:at + HD], lat).astype(BF)
-        duv_ref[i] = dot_tn(lat, sum_ref[0, :, at + HD:at + 2 * HD]).astype(BF)
+    for pair in range(STEP // 2):
+        for i in range(2):
+            at = 2 * i * HD
+            duk_ref[2 * pair + i] = dot_tn(sum_ref[pair, :, at:at + HD], lat).astype(BF)
+            duv_ref[2 * pair + i] = dot_nn(
+                lat_t[...], sum_ref[pair, :, at + HD:at + 2 * HD]
+            ).astype(BF)
 
 
 def weight_grads(summed, lat_all):
     pairs, rows, wide = summed.shape
     return pl.pallas_call(
         weights_kernel,
-        grid=(pairs,),
+        grid=(2 * pairs // STEP,),
         in_specs=[
-            pl.BlockSpec((1, rows, wide), lambda i: (i, 0, 0)),
+            pl.BlockSpec((STEP // 2, rows, wide), lambda i: (i, 0, 0)),
             pl.BlockSpec((rows, LAT), lambda i: (0, 0)),
         ],
         out_specs=[
-            pl.BlockSpec((2, HD, LAT), lambda i: (i, 0, 0)),
-            pl.BlockSpec((2, LAT, HD), lambda i: (i, 0, 0)),
+            pl.BlockSpec((STEP, HD, LAT), lambda i: (i, 0, 0)),
+            pl.BlockSpec((STEP, LAT, HD), lambda i: (i, 0, 0)),
         ],
         out_shape=[
             jax.ShapeDtypeStruct((2 * pairs, HD, LAT), BF),
             jax.ShapeDtypeStruct((2 * pairs, LAT, HD), BF),
         ],
+        scratch_shapes=[pltpu.VMEM((LAT, rows), BF)],
         compiler_params=pltpu.CompilerParams(vmem_limit_bytes=32 * 2**20),
     )(summed, lat_all)
 
@@ -377,13 +393,8 @@
     keys = jnp.take(
         table.reshape(rows // P_SIZE, P_SIZE, LAT + ROPE), blocks, axis=0
     ).reshape(-1, LAT + ROPE)
-    rope = keys[:, LAT:]
-    none = jnp.zeros_like(rope)
-    rope2 = jnp.stack(
-        [jnp.concatenate([rope, none], axis=1), jnp.concatenate([none, rope], axis=1)]
-    )
-    d_nope, d_rope, dkv, dc, dr = local_part(
-        live_rows[0], q_nope, q_rope, grad_out, w_uk, w_uv, keys[:, :LAT], rope2
+    d_nope, d_rope, dkv, d_keys = local_part(
+        live_rows[0], q_nope, q_rope, grad_out, w_uk, w_uv, keys
     )
 
     def rows_of(which):
@@ -391,7 +402,6 @@
         at = at.reshape(which.shape[:-1] + (-1,))
         return jnp.arange(rows)[:, None] == at[..., None, :]
 
-    d_keys = jnp.concatenate([dc, dr[0, :, :ROPE] + dr[1, :, ROPE:]], axis=1)
     select = rows_of(blocks)
     partial_rows = jnp.dot(select.astype(F32), d_keys, precision=lax.Precision.HIGHEST)
     if pairs == n == 2 * CHIPS:

time: 89.4 us -> 86.1 us (0.963)
  local copies, waits for them, and re-layouts: 8.27 us -> 3.9 us
  matrix products: 0.46 us -> 1.43 us
    unnamed x19 -> x5, local copies, waits for them, and re-layouts: 6.14 us -> 1.86 us
    dot_general x1, matrix products: 0.46 us -> 1.43 us  [per_device(): jnp.dot(select.astype(F32), d_keys, precision=lax.Precision.HIGHEST)]
where the time goes in v3:
time: 86.1 us; the launch traced here: 85.8 us
  Pallas kernels  77.4 us (90%)
  local copies, waits for them, and re-layouts  3.9 us (5%)
  other arithmetic  2.38 us (3%)
  matrix products  1.43 us (2%)
    pallas_call x1, Pallas kernels, sum_parts(): pl.pallas_call(functools.partial(sum_kernel, n, nh), out_shape=[jax.Shape...  44 us
    pallas_call x1, Pallas kernels, local_part(): pl.pallas_call(local_kernel, grid=(heads // STEP,), in_specs=[pl.BlockSpe...  18 us
    pallas_call x1, Pallas kernels, gather_blocks(): pl.pallas_call(functools.partial(gather_kernel, n), out_shape=jax.ShapeDt...  11.7 us
    pallas_call x1, Pallas kernels, weight_grads(): pl.pallas_call(weights_kernel, grid=(2 * pairs // STEP,), in_specs=[pl.Bl...  3.68 us
    unnamed x5, local copies, waits for them, and re-layouts  1.86 us

profile of v3, /device:TPU:0, one launch (start us, length us, event | category | flops | bytes accessed | tf_op | source)
XLA Modules:
  0.0 85.8 jit_solution(15661509066417597401)
XLA Ops:
  0.6 0.0 copy-start
  0.6 0.7 fusion.4
  1.3 0.1 add.79
  1.4 0.0 copy-done
  1.4 0.6 gather_fusion
  2.1 0.1 broadcast_in_dim.21
  2.1 0.1 broadcast_in_dim.22
  2.2 0.1 add.76
  2.3 0.1 add.77
  2.4 0.8 fusion.3.mine_ref
  3.2 11.7 %shard_map.128 = bf16[8,48,576]{2,1,0:T(8,128)(2,1)S(1)} custom-call(bf16[48,576]{1,0:T(8,128)(2,1)S(1)} %fusion.3.mine_ref), custom_call_target="tpu_custom_call" | custom-call | tf_op jit(solution)/shard_map/pallas_call | solution.py:194
  14.9 0.1 add.81
  15.0 0.1 add.82
  15.1 0.6 gather_fusion.1
  15.7 0.8 bitcast_select_fusion.keys_ref
  16.4 0.1 fusion.sel_ref
  16.6 18.0 %shard_map.129 = (bf16[256,2048]{1,0:T(8,128)(2,1)}, bf16[256,1024]{1,0:T(8,128)(2,1)}, bf16[8,128,512]{2,1,0:T(8,128)(2,1)}, f32[128,576]{1,0:T(8,128)}) custom-call(s32[4]{0:T(128)} %bitcast.22, bf16[256,2048]{1,0:T(8,128)(2,1)} %qn_ref.1, bf16[256,1024]{1,0:T(8,128)(2,1)} %qr_ref.1, bf16[256,2048]{1,0:T(8,128)(2,1)} %go_ref.1, ...), custom_call_target="tpu_custom_call" | custom-call | tf_op jit(solution)/shard_map/pallas_call | solution.py:101
  34.6 1.4 %convolution_convert_fusion = bf16[256,576]{0,1:T(8,128)(2,1)S(1)} fusion(f32[128,576]{1,0:T(8,128)} %get-tuple-element.28, s32[128]{0:T(128)S(1)} %add.80), kind=kOutput, calls=%fused_computation.2 | convolution fusion | flops 226672640 | bytes 590336 | tf_op jit(solution)/shard_map/dot_general | solution.py:406
  36.0 0.2 copy.20
  36.2 0.0 copy-start.1
  36.2 1.2 %copy-done.1 = bf16[8,128,512]{2,1,0:T(8,128)(2,1)S(1)} copy-done((bf16[8,128,512]{2,1,0:T(8,128)(2,1)S(1)}, bf16[8,128,512]{2,1,0:T(8,128)(2,1)}, u32[]{:S(2)}) %copy-start.1) | copy-done | bytes 1048600
  37.4 44.0 %shard_map.130 = (bf16[16,128,512]{2,1,0:T(8,128)(2,1)S(1)}, f32[32,576]{1,0:T(8,128)S(1)}) custom-call(bf16[8,128,512]{2,1,0:T(8,128)(2,1)S(1)} %copy-done.1, bf16[8,32,576]{2,1,0:T(8,128)(2,1)S(1)} %bitcast.19, bf16[8,256,128]{2,1,0:T(8,128)(2,1)S(1)} %fusion.sel_ref), custom_call_target="tpu_custom_call" | custom-call | tf_op jit(solution)/shard_map/pallas_call | solution.py:322
  81.5 3.7 %shard_map.131 = (bf16[16,128,512]{2,1,0:T(8,128)(2,1)}, bf16[16,512,128]{2,1,0:T(8,128)(2,1)}) custom-call(bf16[8,256,512]{2,1,0:T(8,128)(2,1)S(1)} %bitcast.18, bf16[256,512]{1,0:T(8,128)(2,1)S(1)} %slice.32.lat_ref), custom_call_target="tpu_custom_call" | custom-call | tf_op jit(solution)/shard_map/pallas_call | solution.py:361
  85.2 0.6 copy.25
  (11 shorter events, 0.1 us)
Async XLA Ops:
  0.6 0.8 copy-start
  36.2 1.2 %copy-start.1 = (bf16[8,128,512]{2,1,0:T(8,128)(2,1)S(1)}, bf16[8,128,512]{2,1,0:T(8,128)(2,1)}, u32[]{:S(2)}) copy-start(bf16[8,128,512]{2,1,0:T(8,128)(2,1)} %get-tuple-element.27.dkv_ref) | copy-start | bytes 3145732
